TPU v7x, 256 devices: a whole 4x4x8 slice. The times are simulated.
256 devices in a mesh: dp: 16 (over x, z_hi, core), ctx: 16 (over y, z_lo).
Axes of the slice: x: 4, y: 4, z: 8 (z_hi: 2, z_lo: 4; z = z_hi * 4 + z_lo), core: 2. Of those that a mesh axis runs over, the one named last changes fastest.
Arguments:
- saved_input: bfloat16 [16, 4096, 2048], P('dp', None, 'ctx'), may hold values from -6 to 6
- out_gate: bfloat16 [16, 4096, 2048], P('dp', None, 'ctx'), may hold values from -6 to 6
- grad_out: bfloat16 [16, 4096, 2048], P('dp', None, 'ctx'), may hold values from -6 to 6
- long_filter: float32 [4096, 2048], P('ctx'), may hold values from -0.125 to 0.125
Outputs:
- grad_input: bfloat16 [16, 4096, 2048], P('dp', None, 'ctx')
- grad_filter: float32 [4096, 2048], P('ctx', 'dp')
All inputs are finite; a program needn't handle non-finite values.
Results may differ from a plain program's by a relative error of at most 0.0085.
Values may be sent and summed in bfloat16 or wider, within the bound.
A program may use at most 128 MiB of HBM per device.

v0:
```python
import math

import jax
import jax.numpy as jnp
from jax import lax
from jax.sharding import PartitionSpec as P

RADIX = 128


def exact_product(form, left, right):
    return jnp.einsum(form, left, right, precision=lax.Precision.HIGH)


def phase_table(rows_count, cols_count, period, row_offset, col_offset):
    row_index = lax.broadcasted_iota(jnp.int32, (rows_count, cols_count), 0) + row_offset
    col_index = lax.broadcasted_iota(jnp.int32, (rows_count, cols_count), 1) + col_offset
    product_mod = row_index * col_index % period
    angles = product_mod.astype(jnp.float32) * (2.0 * math.pi / period)
    return (jnp.cos(angles), jnp.sin(angles))


def swap_halves(stacked):
    return jnp.concatenate([stacked[..., RADIX:], stacked[..., :RADIX]], axis=-1)


def apply_twist(stacked, rows_here, points, row_offset, sign):
    twist_cos, twist_sin = phase_table(rows_here, RADIX, points, row_offset, 0)
    gain = jnp.concatenate([twist_cos, twist_cos], axis=-1)
    cross = jnp.concatenate([sign * twist_sin, -sign * twist_sin], axis=-1)
    return stacked * gain + swap_halves(stacked) * cross


def mixing_matrix(sign):
    last_cos, last_sin = phase_table(RADIX, RADIX, RADIX, 0, 0)
    upper = jnp.concatenate([last_cos, -sign * last_sin], axis=1)
    lower = jnp.concatenate([sign * last_sin, last_cos], axis=1)
    return jnp.concatenate([upper, lower], axis=0)


def forward_spectrum(signal):
    channels, length = signal.shape
    half_rows = length // RADIX
    rows_all = 2 * half_rows
    points = 2 * length
    blocked = signal.reshape(channels, half_rows, RADIX)
    first_cos, first_sin = phase_table(rows_all, half_rows, rows_all, 0, 0)
    first_table = jnp.stack([first_cos, -first_sin])
    section = exact_product("pkn,cnm->ckpm", first_table, blocked).reshape(
        channels, rows_all, 2 * RADIX
    )
    twisted = apply_twist(section, rows_all, points, 0, 1.0)
    return exact_product("ckn,nm->ckm", twisted, mixing_matrix(1.0))


def inverse_first(spec, row_offset, points):
    rows_here = spec.shape[1]
    inner = exact_product("ckn,nm->ckm", spec, mixing_matrix(-1.0))
    return apply_twist(inner, rows_here, points, row_offset, -1.0)


def back_table(span_rows, rows_here, rows_all, row_begin, col_offset):
    back_cos, back_sin = phase_table(span_rows, rows_here, rows_all, row_begin, col_offset)
    return jnp.stack([back_cos, -back_sin], axis=-1)


def inverse_second(outer, row_begin, span_rows, col_offset, rows_all, points):
    channels, rows_here = (outer.shape[0], outer.shape[1])
    table = back_table(span_rows, rows_here, rows_all, row_begin, col_offset)
    split = outer.reshape(channels, rows_here, 2, RADIX)
    return exact_product("nkp,ckpm->cnm", table, split) * (1.0 / points)


def on_device(saved_input, out_gate, grad_out, long_filter):
    conv_grad = (out_gate.astype(jnp.float32) * grad_out.astype(jnp.float32)).astype(jnp.bfloat16)
    moved_input, moved_grad = (
        lax.all_to_all(saved_input, "ctx", split_axis=1, concat_axis=2, tiled=True),
        lax.all_to_all(conv_grad, "ctx", split_axis=1, concat_axis=2, tiled=True),
    )
    signal_input = moved_input[0].astype(jnp.float32)
    signal_grad = moved_grad[0].astype(jnp.float32)
    channels, length = signal_input.shape
    half_rows = length // RADIX
    rows_all = 2 * half_rows
    points = 2 * length
    grad_scale = 1.0 / math.sqrt(lax.axis_size("dp") * length)
    input_spec = forward_spectrum(signal_input)
    grad_spec = forward_spectrum(signal_grad)
    taps_spec = forward_spectrum(long_filter)
    input_real, input_imag = (input_spec[..., :RADIX], input_spec[..., RADIX:])
    grad_real, grad_imag = (grad_spec[..., :RADIX], grad_spec[..., RADIX:])
    taps_real, taps_imag = (taps_spec[..., :RADIX], taps_spec[..., RADIX:])
    back_spec = jnp.concatenate(
        [
            taps_real * grad_real + taps_imag * grad_imag,
            taps_real * grad_imag - taps_imag * grad_real,
        ],
        axis=-1,
    )
    outer = inverse_first(back_spec, 0, points)
    signal_back = inverse_second(outer, 0, half_rows, 0, rows_all, points)
    grad_channels = signal_back.reshape(1, channels, length).astype(jnp.bfloat16)
    grad_input = lax.all_to_all(grad_channels, "ctx", split_axis=2, concat_axis=1, tiled=True)
    cross_spec = jnp.concatenate(
        [
            grad_real * input_real + grad_imag * input_imag,
            grad_imag * input_real - grad_real * input_imag,
        ],
        axis=-1,
    )
    cross_outer = inverse_first(cross_spec, 0, points)
    own_filter = inverse_second(cross_outer, 0, half_rows, 0, rows_all, points)
    own_filter = own_filter.reshape(channels, length)
    grad_filter = lax.psum_scatter(own_filter, "dp", scatter_dimension=1, tiled=True) * grad_scale
    return (grad_input, grad_filter)


def solution(mesh):
    in_specs = (P("dp", None, "ctx"), P("dp", None, "ctx"), P("dp", None, "ctx"), P("ctx", None))
    out_specs = (P("dp", None, "ctx"), P("ctx", "dp"))
    return jax.shard_map(
        on_device, mesh=mesh, in_specs=in_specs, out_specs=out_specs, check_vma=False
    )
```

profile of v0, /device:TPU:26, one launch (start us, length us, event | category | flops | bytes accessed | tf_op | source)
XLA Modules:
  0.0 374.3 jit_solution(167576812046352840)
XLA Ops:
  7.2 1.8 multiply_convert_fusion
  9.0 16.7 %copy.121 = bf16[1,4096,128]{2,0,1:T(2,128)(2,1)S(1)} copy(bf16[1,4096,128]{2,1,0:T(8,128)(2,1)S(1)} %multiply_convert_fusion) | data formatting | bytes 2097152 | tf_op jit(solution)/shard_map/convert_element_type | solution.py:75
  25.7 0.5 broadcast.253
  26.2 22.4 %reduce.1 = bf16[4096,128]{1,0:T(8,128)(2,1)S(1)} reduce(bf16[4096,1,128]{2,1,0:T(2,128)(2,1)S(1)} %bitcast.107, bf16[]{:T(256)} %broadcast.253), dimensions={1}, to_apply=%bitcast.88.reduce_sub_computation | reduce | bytes 2097154
  48.6 1.1 reshape.193
  49.8 9.4 %all-to-all-start = ((bf16[16,2,16384]{2,1,0:T(2,128)(2,1)}), bf16[16,2,16384]{2,1,0:T(2,128)(2,1)S(1)}, u32[]{:S(2)}, u32[]{:S(2)}) async-start(bf16[16,2,16384]{2,1,0:T(2,128)(2,1)} %reshape.193), calls=%async_computation | async-start | bytes 2097152 | tf_op jit(solution)/shard_map/all_to_all | solution.py:78
  59.1 3.2 copy.120
  62.3 23.4 %reduce = bf16[4096,128]{1,0:T(8,128)(2,1)} reduce(bf16[4096,1,128]{2,1,0:T(2,128)(2,1)S(1)} %bitcast.109, bf16[]{:T(256)} %broadcast.253), dimensions={1}, to_apply=%bitcast.87.reduce_sub_computation | reduce | bytes 2097154
  85.7 2.2 reshape.197
  87.9 2.0 copy.106
  90.0 5.9 %convolution_bitcast_fusion.2 = f32[256,32,2,128]{3,1,0,2:T(8,128)} fusion(f32[256,16,128,1]{2,1,0,3:T(8,128)S(1)} %bitcast.101, f32[1,32,16]{1,2,0:T(8,128)S(1)} %get-tuple-element.22, f32[1,32,16]{1,2,0:T(8,128)S(1)} %get-tuple-element.23), kind=kOutput, calls=%fused_computation.42 | convolution fusion | flops 201327616 | bytes 10489856 | tf_op jit(solution)/shard_map/pkn,cnm->ckpm/dot_general | solution.py:12
  95.8 9.9 %copy.78 = f32[256,32,2,128]{0,3,2,1:T(8,128)} copy(f32[256,32,2,128]{3,1,0,2:T(8,128)} %convolution_bitcast_fusion.2) | data formatting | bytes 16777216 | tf_op jit(solution)/shard_map/pkn,cnm->ckpm/transpose | solution.py:12
  105.9 0.3 fusion.56
  106.2 7.8 %fusion.96 = (f32[256,32,128]{0,2,1:T(8,128)}, f32[256,32,128]{0,2,1:T(8,128)}) fusion(f32[256,32,256]{0,2,1:T(8,128)} %bitcast.89), kind=kLoop, calls=%fused_computation.130 | loop fusion | bytes 16777216 | tf_op jit(solution)/shard_map/slice | solution.py:24
  114.0 7.5 %all-to-all-start.2 = ((bf16[16,2,16384]{2,1,0:T(2,128)(2,1)}), bf16[16,2,16384]{2,1,0:T(2,128)(2,1)}, u32[]{:S(2)}, u32[]{:S(2)}) async-start(bf16[16,2,16384]{2,1,0:T(2,128)(2,1)} %reshape.197), calls=%async_computation.2 | async-start | bytes 2097152 | tf_op jit(solution)/shard_map/all_to_all | solution.py:77
  121.5 0.2 reduce-scatter.2.cloned.1.call-start
  121.8 0.3 broadcast_multiply_fusion.1
  122.1 11.1 %fusion.1 = f32[256,32,256]{0,2,1:T(8,128)} fusion(f32[256,32,128]{0,2,1:T(8,128)} %get-tuple-element.17, f32[256,32,128]{0,2,1:T(8,128)} %get-tuple-element.16, f32[256,32,256]{0,2,1:T(8,128)} %bitcast.90, f32[32,256]{1,0:T(8,128)S(1)} %get-tuple-element.21, f32[32,256]{1,0:T(8,128)S(1)} %pad_maximum_fusion.4, f32[128,128]{0,1:T(8,128)S(1)} %fusion.56, ...), kind=kOutput, calls=%fused_computation.2 | convolution fusion | flops 3229810688 | bytes 25427968 | tf_op jit(solution)/shard_map/ckn,nm->ckm/dot_general | solution.py:12
  133.2 1.0 reshape.194
  134.4 5.7 %convolution_bitcast_fusion.1 = f32[256,32,2,128]{3,1,2,0:T(8,128)} fusion(bf16[1,16,256,128]{3,2,1,0:T(8,128)(2,1)S(1)} %bitcast.111, f32[1,32,16]{1,2,0:T(8,128)S(1)} %get-tuple-element.22, f32[1,32,16]{1,2,0:T(8,128)S(1)} %get-tuple-element.23), kind=kOutput, calls=%fused_computation.41 | convolution fusion | flops 201327616 | bytes 9441280 | tf_op jit(solution)/shard_map/pkn,cnm->ckpm/dot_general | solution.py:12
  140.1 9.9 %copy.82 = f32[256,32,2,128]{0,3,2,1:T(8,128)} copy(f32[256,32,2,128]{3,1,2,0:T(8,128)} %convolution_bitcast_fusion.1) | data formatting | bytes 16777216 | tf_op jit(solution)/shard_map/pkn,cnm->ckpm/transpose | solution.py:12
  150.1 7.8 %fusion.95 = (f32[256,32,128]{0,2,1:T(8,128)}, f32[256,32,128]{0,2,1:T(8,128)}) fusion(f32[256,32,256]{0,2,1:T(8,128)} %bitcast.91), kind=kLoop, calls=%fused_computation.129 | loop fusion | bytes 16777216 | tf_op jit(solution)/shard_map/slice | solution.py:24
  157.9 4.3 %reshape.198 = bf16[4096,1,128]{2,1,0:T(2,128)(2,1)S(1)} reshape(bf16[16,2,16384]{2,1,0:T(2,128)(2,1)} %all-to-all-done.2) | data formatting | bytes 2097152
  162.3 6.1 %convolution_bitcast_fusion = f32[256,32,2,128]{3,1,0,2:T(8,128)} fusion(bf16[1,16,256,128]{3,2,1,0:T(8,128)(2,1)S(1)} %bitcast.110, f32[1,32,16]{1,2,0:T(8,128)S(1)} %get-tuple-element.22, f32[1,32,16]{1,2,0:T(8,128)S(1)} %get-tuple-element.23), kind=kOutput, calls=%fused_computation.40 | convolution fusion | flops 201327616 | bytes 9441280 | tf_op jit(solution)/shard_map/pkn,cnm->ckpm/dot_general | solution.py:12
  168.4 9.9 %copy.90 = f32[256,32,2,128]{0,3,2,1:T(8,128)} copy(f32[256,32,2,128]{3,1,0,2:T(8,128)} %convolution_bitcast_fusion) | data formatting | bytes 16777216 | tf_op jit(solution)/shard_map/pkn,cnm->ckpm/transpose | solution.py:12
  178.3 7.9 %fusion.93 = (f32[256,32,128]{0,2,1:T(8,128)}, f32[256,32,128]{0,2,1:T(8,128)}) fusion(f32[256,32,256]{0,2,1:T(8,128)} %bitcast.93), kind=kLoop, calls=%fused_computation.127 | loop fusion | bytes 16777216 | tf_op jit(solution)/shard_map/slice | solution.py:24
  186.3 12.8 %fusion.6 = f32[256,32,256]{0,2,1:T(8,128)} fusion(f32[256,32,128]{0,2,1:T(8,128)} %get-tuple-element.15, f32[256,32,128]{0,2,1:T(8,128)S(1)} %copy-done, f32[256,32,256]{0,2,1:T(8,128)} %bitcast.92, f32[32,256]{1,0:T(8,128)S(1)} %get-tuple-element.21, f32[32,256]{1,0:T(8,128)S(1)} %pad_maximum_fusion.4, f32[128,128]{0,1:T(8,128)S(1)} %fusion.56, ...), kind=kOutput, calls=%fused_computation.7 | convolution fusion | flops 3229810688 | bytes 25427968 | tf_op jit(solution)/shard_map/ckn,nm->ckm/dot_general | solution.py:12
  199.1 10.5 %fusion.16 = f32[256,32,256]{0,2,1:T(8,128)} fusion(f32[256,32,128]{0,2,1:T(8,128)} %get-tuple-element.11, f32[256,32,128]{0,2,1:T(8,128)} %get-tuple-element.10, f32[256,32,256]{0,2,1:T(8,128)S(1)} %bitcast.96, f32[32,256]{1,0:T(8,128)S(1)} %get-tuple-element.21, f32[32,256]{1,0:T(8,128)S(1)} %pad_maximum_fusion.4, f32[128,128]{0,1:T(8,128)S(1)} %fusion.56, ...), kind=kOutput, calls=%fused_computation.18 | convolution fusion | flops 3229810688 | bytes 25427968 | tf_op jit(solution)/shard_map/ckn,nm->ckm/dot_general | solution.py:12
  209.6 11.2 %multiply_add_fusion = (f32[256,32,128]{0,2,1:T(8,128)}, f32[256,32,128]{0,2,1:T(8,128)}, f32[256,32,128]{0,2,1:T(8,128)S(1)}, f32[256,32,128]{0,2,1:T(8,128)}) fusion(f32[256,32,256]{0,2,1:T(8,128)} %fusion.16, f32[256,32,256]{0,2,1:T(8,128)} %fusion.6, f32[256,32,256]{0,2,1:T(8,128)S(1)} %bitcast.98), kind=kLoop, calls=%fused_computation.31 | loop fusion | flops 12582912 | bytes 41943040 | tf_op jit(solution)/shard_map/add | solution.py:106
  220.8 6.3 %fusion.10 = f32[256,32,256]{0,2,1:T(8,128)S(1)} fusion(f32[256,32,128]{0,2,1:T(8,128)S(1)} %get-tuple-element.8, f32[256,32,128]{0,2,1:T(8,128)} %get-tuple-element.9, f32[128,128]{0,1:T(8,128)S(1)} %fusion.56, f32[128,128]{0,1:T(8,128)S(1)} %get-tuple-element.26, f32[128,128]{0,1:T(8,128)S(1)} %get-tuple-element.27), kind=kOutput, calls=%fused_computation.10 | convolution fusion | flops 3223519232 | bytes 16973824 | tf_op jit(solution)/shard_map/ckn,nm->ckm/dot_general | solution.py:12
  227.1 2.7 fusion.94
  229.8 6.2 %fusion.20 = f32[256,32,256]{0,2,1:T(8,128)S(1)} fusion(f32[256,32,128]{0,2,1:T(8,128)} %get-tuple-element.3, f32[256,32,128]{0,2,1:T(8,128)} %get-tuple-element.2, f32[128,128]{0,1:T(8,128)S(1)} %fusion.56, f32[128,128]{0,1:T(8,128)S(1)} %get-tuple-element.26, f32[128,128]{0,1:T(8,128)S(1)} %get-tuple-element.27), kind=kOutput, calls=%fused_computation.21 | convolution fusion | flops 3223519232 | bytes 16973824 | tf_op jit(solution)/shard_map/ckn,nm->ckm/dot_general | solution.py:12
  236.1 3.8 %fusion.92 = (f32[256,32,128]{0,2,1:T(8,128)}, f32[256,32,128]{0,2,1:T(8,128)}) fusion(f32[256,32,256]{0,2,1:T(8,128)S(1)} %fusion.20), kind=kLoop, calls=%fused_computation.126 | loop fusion | bytes 16777216 | tf_op jit(solution)/shard_map/slice | solution.py:24
  239.9 11.2 %fusion.24 = (f32[256,32,256]{0,2,1:T(8,128)}, f32[256,32,256]{0,2,1:T(8,128)}) fusion(f32[256,32,128]{0,2,1:T(8,128)} %get-tuple-element.7, f32[256,32,128]{0,2,1:T(8,128)} %get-tuple-element.6, f32[256,32,256]{0,2,1:T(8,128)S(1)} %fusion.20, f32[32,256]{1,0:T(8,128)S(1)} %get-tuple-element.20, f32[32,256]{1,0:T(8,128)S(1)} %pad_maximum_fusion.4, ...), kind=kLoop, calls=%fused_computation.26 | loop fusion | flops 16777216 | bytes 50397184 | tf_op jit(solution)/shard_map/add | solution.py:31
  251.1 10.5 %copy.93 = f32[256,32,2,128]{3,1,2,0:T(8,128)} copy(f32[256,32,2,128]{0,3,2,1:T(8,128)} %bitcast.100) | data formatting | bytes 16777216 | tf_op jit(solution)/shard_map/reshape | solution.py:70
  261.6 4.9 %bitcast_multiply_fusion = f32[256,128,16]{1,2,0:T(8,128)S(1)} fusion(f32[256,32,2,128]{3,1,2,0:T(8,128)} %copy.93, f32[16,32,1]{1,0,2:T(8,128)S(1)} %get-tuple-element.28, f32[16,32,1]{1,0,2:T(8,128)S(1)} %get-tuple-element.29), kind=kOutput, calls=%fused_computation.44 | convolution fusion | flops 201851904 | bytes 10489856 | tf_op jit(solution)/shard_map/nkp,ckpm->cnm/dot_general | solution.py:12
  266.4 2.2 copy.119
  268.7 10.5 %copy.85 = f32[256,32,2,128]{3,1,2,0:T(8,128)} copy(f32[256,32,2,128]{0,3,2,1:T(8,128)} %bitcast.99) | data formatting | bytes 16777216 | tf_op jit(solution)/shard_map/reshape | solution.py:70
  279.2 5.6 %fusion.35 = bf16[256,16,128]{2,1,0:T(8,128)(2,1)S(1)} fusion(f32[256,32,2,128]{3,1,2,0:T(8,128)} %copy.85, f32[16,32,1]{1,0,2:T(8,128)S(1)} %get-tuple-element.28, f32[16,32,1]{1,0,2:T(8,128)S(1)} %get-tuple-element.29), kind=kOutput, calls=%fused_computation.48 | convolution fusion | flops 202376192 | bytes 9441280 | tf_op jit(solution)/shard_map/nkp,ckpm->cnm/dot_general | solution.py:12
  284.9 0.5 convert_element_type.110
  285.4 1.7 copy.86
  287.1 10.6 %reduce.2 = bf16[2048,256]{1,0:T(8,128)(2,1)S(1)} reduce(bf16[2048,1,256]{2,1,0:T(2,128)(2,1)S(1)} %bitcast.108, bf16[]{:T(256)} %broadcast.253), dimensions={1}, to_apply=%bitcast.77.reduce_sub_computation | reduce | bytes 2097154
  297.7 0.3 reshape.195
  298.0 42.8 %all_to_all.48 = bf16[16,2,16384]{2,1,0:T(2,128)(2,1)S(1)} all-to-all(bf16[16,2,16384]{2,1,0:T(2,128)(2,1)S(1)} %reshape.195), channel_id=1, replica_groups=mesh['dp'=16,'ctx'=16] {'ctx'}, dimensions={0} | all-to-all | bytes 2097152 | tf_op jit(solution)/shard_map/all_to_all | solution.py:103
  340.8 1.0 reshape.196
  342.0 1.3 copy.87
  343.3 22.1 %reduce-scatter.2.cloned.1.call-done = f32[256,128]{1,0:T(8,128)} async-done(((f32[256,2048]{1,0:T(8,128)}), f32[256,128]{1,0:T(8,128)}) %reduce-scatter.2.cloned.1.call-update) | async-done | bytes 131088 | tf_op jit(solution)/shard_map/reduce_scatter | solution.py:114
  365.4 1.6 broadcast_multiply_fusion
  (24 shorter events, 0.8 us)
Async XLA Ops:
  49.8 64.3 %all-to-all-start = ((bf16[16,2,16384]{2,1,0:T(2,128)(2,1)}), bf16[16,2,16384]{2,1,0:T(2,128)(2,1)S(1)}, u32[]{:S(2)}, u32[]{:S(2)}) async-start(bf16[16,2,16384]{2,1,0:T(2,128)(2,1)} %reshape.193), calls=%async_computation | async-start | bytes 2097152 | tf_op jit(solution)/shard_map/all_to_all | solution.py:78
  114.0 43.8 %all-to-all-start.2 = ((bf16[16,2,16384]{2,1,0:T(2,128)(2,1)}), bf16[16,2,16384]{2,1,0:T(2,128)(2,1)}, u32[]{:S(2)}, u32[]{:S(2)}) async-start(bf16[16,2,16384]{2,1,0:T(2,128)(2,1)} %reshape.197), calls=%async_computation.2 | async-start | bytes 2097152 | tf_op jit(solution)/shard_map/all_to_all | solution.py:77
  121.5 243.9 %reduce-scatter.2.cloned.1.call-start = ((), (), s32[]{:S(2)}) async-start(), calls=%async_computation.4 | async-start | bytes 2228224 | tf_op jit(solution)/shard_map/reduce_scatter | solution.py:114
  178.3 7.9 %copy-start = (f32[256,32,128]{0,2,1:T(8,128)S(1)}, f32[256,32,128]{0,2,1:T(8,128)}, u32[]{:S(2)}) copy-start(f32[256,32,128]{0,2,1:T(8,128)} %get-tuple-element.14) | copy-start | bytes 12582916
  178.3 20.7 %slice-start = ((s8[8388608]{0:T(1024)(128)(4,1)}), s8[4194304]{0:T(1024)(128)(4,1)S(1)}, s32[]{:S(2)}) async-start(s8[8388608]{0:T(1024)(128)(4,1)} %bitcast.94), calls=%async_computation.5 | async-start | bytes 8388608
  186.2 12.8 %slice-start.1 = ((s8[8388608]{0:T(1024)(128)(4,1)}), s8[4194304]{0:T(1024)(128)(4,1)S(1)}, s32[]{:S(2)}) async-start(s8[8388608]{0:T(1024)(128)(4,1)} %bitcast.94), calls=%async_computation.6 | async-start | bytes 8388608
  186.3 23.3 %slice-start.2 = ((s8[8388608]{0:T(1024)(128)(4,1)}), s8[4194304]{0:T(1024)(128)(4,1)S(1)}, s32[]{:S(2)}) async-start(s8[8388608]{0:T(1024)(128)(4,1)} %bitcast.97), calls=%async_computation.7 | async-start | bytes 8388608
  199.1 10.5 %slice-start.3 = ((s8[8388608]{0:T(1024)(128)(4,1)}), s8[4194304]{0:T(1024)(128)(4,1)S(1)}, s32[]{:S(2)}) async-start(s8[8388608]{0:T(1024)(128)(4,1)} %bitcast.97), calls=%async_computation.8 | async-start | bytes 8388608
Sparse Core Ops, SparseCore 0:
  268.8 96.5 reduce-scatter.1
where the time goes:
time: 381 us; the launch traced here: 374 us
  local copies, waits for them, and re-layouts  119 us (31%)
  other arithmetic  83 us (22%)
  matrix products  75.1 us (20%)
  blocking collectives  42.8 us (11%)
  waiting for transfers between devices  22.1 us (6%)
  starting transfers between devices  17.1 us (4%)
  between operations  14.7 us (4%)
    dot_general x10, matrix products, exact_product(): return jnp.einsum(form, left, right, precision=lax.Precision.HIGH)  75.1 us
    unnamed x5, other arithmetic  56.4 us
    all_to_all x1, blocking collectives, on_device(): lax.all_to_all(grad_channels, 'ctx', split_axis=2, concat_axis=1, tiled=T...  42.8 us
    slice x5, local copies, waits for them, and re-layouts, swap_halves(): stacked[..., RADIX:]  30.1 us
    transpose x3, local copies, waits for them, and re-layouts, exact_product(): return jnp.einsum(form, left, right, precision=lax.Precision.HIGH)  29.7 us
    reduce_scatter x1, waiting for transfers between devices, on_device(): lax.psum_scatter(own_filter, 'dp', scatter_dimension=1, tiled=True)  22.1 us
    reshape x2, local copies, waits for them, and re-layouts, inverse_second(): split = outer.reshape(channels, rows_here, 2, RADIX)  21 us
    unnamed x23, local copies, waits for them, and re-layouts  18.4 us
  transfers between devices with their start and end apart: 3, of which 1 were waited for; matrix products, arithmetic and copies ran while one was open for 33% of the time, Pallas kernels for 0%

commit v1 on v0

v1 whole, which is shorter than its diff:
```python
import math

import jax
import jax.numpy as jnp
import numpy as np
from jax import lax
from jax.experimental import pallas as pl
from jax.experimental.pallas import tpu as pltpu
from jax.sharding import PartitionSpec as P

MESH = pl.DeviceIdType.MESH
LANES = 128
ROWS = 16
CHUNKS = 4
F32 = jnp.float32
BF16 = jnp.bfloat16


def twiddled_tables():
    k = np.arange(ROWS)[:, None, None]
    n = np.arange(LANES)[None, :, None]
    m = np.arange(LANES)[None, None, :]
    points = 2 * ROWS * LANES
    turns = (n * (2 * (k + 2 * ROWS * m) + 1)) % (2 * points)
    angle = turns * (math.pi / points)
    cos, sin = np.cos(angle), np.sin(angle)
    ahead = np.concatenate(
        [np.concatenate([cos, -sin], axis=2), np.concatenate([sin, cos], axis=2)], axis=1
    )
    return ahead.astype(BF16), np.swapaxes(ahead, 1, 2).astype(BF16)


def split_rows(rows):
    count = len(rows)
    if count == 2:
        turned = rows[1] * math.cos(math.pi / 4)
        return [(rows[0] + turned, -turned), (rows[0] - turned, -turned)]
    even, odd = split_rows(rows[0::2]), split_rows(rows[1::2])
    out = [None] * count
    for k in range(count // 2):
        angle = math.pi * (2 * k + 1) / (2 * count)
        wr, wi = math.cos(angle), -math.sin(angle)
        (er, ei), (pr, pi) = even[k], odd[k]
        tr, ti = wr * pr - wi * pi, wr * pi + wi * pr
        out[k] = (er + tr, ei + ti)
        out[count - 1 - k] = (er - tr, ti - ei)
    return out


def merge_rows(spec):
    count = len(spec)
    if count == 2:
        (a, b), (c, d) = spec
        return [a + c, (a - c - b - d) * math.cos(math.pi / 4)]
    even, odd = [], []
    for k in range(count // 2):
        angle = math.pi * (2 * k + 1) / (2 * count)
        wr, wi = math.cos(angle), -math.sin(angle)
        (pr, pi), (qr, qi) = spec[k], spec[count - 1 - k]
        dr, di = pr - qr, pi + qi
        even.append((pr + qr, pi - qi))
        odd.append((wr * dr + wi * di, wr * di - wi * dr))
    out = [None] * count
    out[0::2], out[1::2] = merge_rows(even), merge_rows(odd)
    return out


def kernel(
    scale,
    u_ref, a_ref, b_ref, h_ref, ahead_ref, back_ref,
    y_ref, f_ref,
    a_buf, b_buf, g_buf, h_buf, u_recv, g_recv, h_first, h_spec, first, last, y_buf,
    f_buf, f_recv1, f_send2, f_recv2, f_send3, f_recv3,
    local_sem, u_send, u_sem, g_send, g_sem, y_send, y_sem,
    s1, r1, s2, r2, s3, r3,
):
    own = f_ref.shape[0]
    size = own // CHUNKS
    dp, me = lax.axis_index("dp"), lax.axis_index("ctx")
    core, z_hi, x = dp % 2, (dp // 2) % 2, dp // 4

    def at_x(step):
        return ((x ^ step) * 4 + z_hi * 2 + core, me)

    other_core = (dp + 1 - 2 * core, me)
    other_z = (dp + 2 - 4 * z_hi, me)

    loads = [
        pltpu.make_async_copy(a_ref, a_buf, local_sem.at[0]),
        pltpu.make_async_copy(b_ref, b_buf, local_sem.at[1]),
        pltpu.make_async_copy(h_ref, h_buf, local_sem.at[2]),
        pltpu.make_async_copy(u_ref.at[pl.ds(me * own, own)], u_recv.at[me], local_sem.at[3]),
    ]
    for copy in loads:
        copy.start()

    barrier = pltpu.get_barrier_semaphore()

    @pl.loop(1, ROWS)
    def _(step):
        pl.semaphore_signal(barrier, inc=1, device_id=(dp, me ^ step), device_id_type=MESH)

    for peer in [other_core, other_z] + [at_x(step) for step in (1, 2, 3)]:
        pl.semaphore_signal(barrier, inc=1, device_id=peer, device_id_type=MESH)

    loads[0].wait()
    loads[1].wait()

    @pl.loop(0, ROWS)
    def _(at):
        rows = pl.ds(at * own, own)
        g_buf[rows] = (a_buf[rows].astype(F32) * b_buf[rows].astype(F32)).astype(BF16)

    keep_g = pltpu.make_async_copy(g_buf.at[pl.ds(me * own, own)], g_recv.at[me], local_sem.at[4])
    keep_g.start()
    pl.semaphore_wait(barrier, ROWS - 1 + 5)

    def exchange(src, dst, send, recv, chunk, step):
        return pltpu.make_async_remote_copy(
            src_ref=src.at[pl.ds((me ^ step) * own + chunk * size, size)],
            dst_ref=dst.at[me, pl.ds(chunk * size, size)],
            send_sem=send.at[chunk, step],
            recv_sem=recv.at[chunk, step],
            device_id=(dp, me ^ step),
            device_id_type=MESH,
        )

    def move_u(chunk, step):
        return exchange(u_ref, u_recv, u_send, u_sem, chunk, step)

    def move_g(chunk, step):
        return exchange(g_buf, g_recv, g_send, g_sem, chunk, step)

    def move_y(chunk, step):
        return pltpu.make_async_remote_copy(
            src_ref=y_buf.at[me ^ step, pl.ds(chunk * size, size)],
            dst_ref=y_ref.at[pl.ds(me * own + chunk * size, size)],
            send_sem=y_send.at[chunk, step],
            recv_sem=y_sem.at[chunk, step],
            device_id=(dp, me ^ step),
            device_id_type=MESH,
        )

    @pl.loop(0, CHUNKS)
    def _(chunk):
        @pl.loop(1, ROWS)
        def _(step):
            move_g(chunk, step).start()
            move_u(chunk, step).start()

    loads[2].wait()

    @pl.loop(0, own // 8)
    def _(at):
        rows = pl.ds(at * 8, 8)
        spec = split_rows([h_buf[rows, j * LANES : (j + 1) * LANES] for j in range(ROWS)])
        for k, (re, im) in enumerate(spec):
            h_first[k, rows, :LANES] = re
            h_first[k, rows, LANES:] = im

    @pl.loop(0, ROWS)
    def _(k):
        h_spec[k] = jnp.dot(
            h_first[k].astype(BF16), ahead_ref[k], preferred_element_type=F32
        ) * (1.0 / (ROWS * LANES))

    loads[3].wait()
    keep_g.wait()

    def compute(chunk):
        base = chunk * size

        @pl.loop(0, size // 16)
        def _(at):
            rows = pl.ds(base + at * 16, 16)
            for place, source in enumerate((g_recv, u_recv)):
                spec = split_rows([source[j, rows].astype(F32) for j in range(ROWS)])
                put = pl.ds(place * size + at * 16, 16)
                for k, (re, im) in enumerate(spec):
                    first[k, put, :LANES] = re.astype(BF16)
                    first[k, put, LANES:] = im.astype(BF16)

        @pl.loop(0, ROWS, unroll=2)
        def _(k):
            spec = jnp.dot(first[k], ahead_ref[k], preferred_element_type=F32)
            gr, gi = spec[:size, :LANES], spec[:size, LANES:]
            ur, ui = spec[size:, :LANES], spec[size:, LANES:]
            hr = h_spec[k, pl.ds(base, size), :LANES]
            hi = h_spec[k, pl.ds(base, size), LANES:]
            to_input = jnp.concatenate([hr * gr + hi * gi, hr * gi - hi * gr], axis=1)
            to_filter = jnp.concatenate([gr * ur + gi * ui, gi * ur - gr * ui], axis=1)
            both = jnp.concatenate([to_input, to_filter], axis=0).astype(BF16)
            last[k] = jnp.dot(both, back_ref[k], preferred_element_type=F32)

        @pl.loop(0, size // 16)
        def _(at):
            rows = pl.ds(base + at * 16, 16)
            for place in range(2):
                take = pl.ds(place * size + at * 16, 16)
                out = merge_rows([(last[k, take, :LANES], last[k, take, LANES:]) for k in range(ROWS)])
                for j in range(ROWS):
                    if place == 0:
                        y_buf[j, rows] = out[j].astype(BF16)
                    else:
                        f_buf[chunk, j % 2, j // 2, pl.ds(at * 16, 16)] = out[j]

    def sum_cores(chunk):
        return pltpu.make_async_remote_copy(
            src_ref=f_buf.at[chunk, 1 - core], dst_ref=f_recv1.at[chunk],
            send_sem=s1.at[chunk], recv_sem=r1.at[chunk],
            device_id=other_core, device_id_type=MESH,
        )

    def sum_x(chunk, step):
        return pltpu.make_async_remote_copy(
            src_ref=f_send2.at[chunk, x ^ step], dst_ref=f_recv2.at[chunk, step],
            send_sem=s2.at[chunk, step], recv_sem=r2.at[chunk, step],
            device_id=at_x(step), device_id_type=MESH,
        )

    def sum_z(chunk):
        return pltpu.make_async_remote_copy(
            src_ref=f_send3.at[chunk], dst_ref=f_recv3.at[chunk],
            send_sem=s3.at[chunk], recv_sem=r3.at[chunk],
            device_id=other_z, device_id_type=MESH,
        )

    def after_cores(chunk):
        sum_cores(chunk).wait()
        for place in range(4):
            for half in range(2):
                at = place * 2 + half
                total = f_buf[chunk, core, at] + f_recv1[chunk, at]
                f_send2[chunk, place, half] = total.astype(BF16)
        for step in (2, 1, 3):
            sum_x(chunk, step).start()

    def held(chunk, half):
        total = f_buf[chunk, core, x * 2 + half] + f_recv1[chunk, x * 2 + half]
        for step in (1, 2, 3):
            total = total + f_recv2[chunk, step, half].astype(F32)
        return total

    def after_x(chunk):
        for step in (1, 2, 3):
            sum_x(chunk, step).wait()
        f_send3[chunk] = held(chunk, 1 - z_hi).astype(BF16)
        sum_z(chunk).start()

    def after_z(chunk):
        sum_z(chunk).wait()
        f_ref[chunk * size : (chunk + 1) * size] = (
            held(chunk, z_hi) + f_recv3[chunk].astype(F32)
        ) * scale

    keeps = []
    for chunk in range(CHUNKS):
        @pl.loop(1, ROWS)
        def _(step):
            move_g(chunk, step).wait_recv()
            move_u(chunk, step).wait_recv()

        compute(chunk)
        sum_cores(chunk).start()

        @pl.loop(1, ROWS)
        def _(step):
            move_y(chunk, step).start()

        keep_y = pltpu.make_async_copy(
            y_buf.at[me, pl.ds(chunk * size, size)],
            y_ref.at[pl.ds(me * own + chunk * size, size)],
            local_sem.at[5 + chunk],
        )
        keep_y.start()
        keeps.append(keep_y)
        if chunk >= 1:
            after_cores(chunk - 1)
        if chunk >= 2:
            after_x(chunk - 2)
        if chunk >= 3:
            after_z(chunk - 3)
    after_cores(CHUNKS - 1)
    after_x(CHUNKS - 2)
    after_x(CHUNKS - 1)
    for chunk in range(CHUNKS - 3, CHUNKS):
        after_z(chunk)

    for keep_y in keeps:
        keep_y.wait()

    @pl.loop(0, CHUNKS)
    def _(chunk):
        @pl.loop(1, ROWS)
        def _(step):
            move_g(chunk, step).wait_send()
            move_u(chunk, step).wait_send()
            move_y(chunk, step).wait()


def on_device(saved_input, out_gate, grad_out, long_filter):
    _, channels, width = saved_input.shape
    own, length = long_filter.shape
    size = own // CHUNKS
    scale = 1.0 / (math.sqrt(lax.axis_size("dp") * length) * ROWS * LANES)
    ahead, back = twiddled_tables()
    in_hbm = pl.BlockSpec(memory_space=pl.ANY)
    in_vmem = pl.BlockSpec(memory_space=pltpu.VMEM)
    dma = pltpu.SemaphoreType.DMA

    def run(*operands):
        return pl.pallas_call(
            lambda *refs: kernel(scale, *refs),
            out_shape=(
                jax.ShapeDtypeStruct((channels, width), BF16),
                jax.ShapeDtypeStruct((own, width), F32),
            ),
            in_specs=[in_hbm] * 4 + [in_vmem] * 2,
            out_specs=(in_hbm, in_vmem),
            scratch_shapes=[
                pltpu.VMEM((channels, width), BF16),
                pltpu.VMEM((channels, width), BF16),
                pltpu.VMEM((channels, width), BF16),
                pltpu.VMEM((own, length), F32),
                pltpu.VMEM((ROWS, own, width), BF16),
                pltpu.VMEM((ROWS, own, width), BF16),
                pltpu.VMEM((ROWS, own, 2 * LANES), F32),
                pltpu.VMEM((ROWS, own, 2 * LANES), F32),
                pltpu.VMEM((ROWS, 2 * size, 2 * LANES), BF16),
                pltpu.VMEM((ROWS, 2 * size, 2 * LANES), F32),
                pltpu.VMEM((ROWS, own, width), BF16),
                pltpu.VMEM((CHUNKS, 2, ROWS // 2, size, LANES), F32),
                pltpu.VMEM((CHUNKS, ROWS // 2, size, LANES), F32),
                pltpu.VMEM((CHUNKS, 4, 2, size, LANES), BF16),
                pltpu.VMEM((CHUNKS, 4, 2, size, LANES), BF16),
                pltpu.VMEM((CHUNKS, size, LANES), BF16),
                pltpu.VMEM((CHUNKS, size, LANES), BF16),
                dma((5 + CHUNKS,)),
                dma((CHUNKS, ROWS)), dma((CHUNKS, ROWS)),
                dma((CHUNKS, ROWS)), dma((CHUNKS, ROWS)),
                dma((CHUNKS, ROWS)), dma((CHUNKS, ROWS)),
                dma((CHUNKS,)), dma((CHUNKS,)),
                dma((CHUNKS, 4)), dma((CHUNKS, 4)),
                dma((CHUNKS,)), dma((CHUNKS,)),
            ],
            compiler_params=pltpu.CompilerParams(
                collective_id=0, has_side_effects=True, vmem_limit_bytes=56 * 2**20
            ),
        )(*operands)

    grad_input, grad_filter = run(
        saved_input[0], out_gate[0], grad_out[0], long_filter, jnp.asarray(ahead), jnp.asarray(back)
    )
    return grad_input[None], grad_filter


def solution(mesh):
    in_specs = (P("dp", None, "ctx"), P("dp", None, "ctx"), P("dp", None, "ctx"), P("ctx", None))
    out_specs = (P("dp", None, "ctx"), P("ctx", "dp"))
    return jax.shard_map(
        on_device, mesh=mesh, in_specs=in_specs, out_specs=out_specs, check_vma=False
    )
```

time: 381 us -> 92.4 us (0.24)
  the two profiles are of different devices: /device:TPU:26 before, /device:TPU:6 now
where the time goes in v1:
time: 92.4 us; the launch traced here: 92.3 us
  Pallas kernels  88.7 us (96%)
  local copies, waits for them, and re-layouts  2.96 us (3%)
    pallas_call x1, Pallas kernels, run(): pl.pallas_call(lambda *refs: kernel(scale, *refs), out_shape=(jax.ShapeDt...  88.7 us
    unnamed x4, local copies, waits for them, and re-layouts  2.96 us

profile of v1, /device:TPU:6, one launch (start us, length us, event | category | flops | bytes accessed | tf_op | source)
XLA Modules:
  0.0 92.3 jit_solution(8284687792282675810)
XLA Ops:
  0.6 88.7 %shard_map.77 = (bf16[4096,128]{1,0:T(8,128)(2,1)}, f32[256,128]{1,0:T(8,128)}) custom-call(bf16[4096,128]{1,0:T(8,128)(2,1)} %bitcast.4, bf16[4096,128]{1,0:T(8,128)(2,1)} %bitcast.5, bf16[4096,128]{1,0:T(8,128)(2,1)} %bitcast.6, f32[256,2048]{1,0:T(8,128)} %refs_3_.1, bf16[16,256,256]{2,1,0:T(8,128)(2,1)} %constant.4.clone.refs_4_, ...), custom_call_target="tpu_custom_call" | custom-call | tf_op jit(solution)/shard_map/pallas_call | solution.py:312
  89.4 0.0 copy-start
  89.4 2.3 %copy.10 = bf16[1,4096,128]{2,1,0:T(8,128)(2,1)} copy(bf16[1,4096,128]{2,1,0:T(8,128)(2,1)} %bitcast.7) | data formatting | bytes 2097152
  91.7 0.0 copy-done
  91.7 0.7 copy.11
Async XLA Ops:
  89.4 2.3 %copy-start = (f32[256,128]{1,0:T(8,128)S(1)}, f32[256,128]{1,0:T(8,128)}, u32[]{:S(2)}) copy-start(f32[256,128]{1,0:T(8,128)} %get-tuple-element.9) | copy-start | bytes 393220

commit v2 on v1

v2 whole, which is shorter than its diff:
```python
import math

import jax
import jax.numpy as jnp
import numpy as np
from jax import lax
from jax.experimental import pallas as pl
from jax.experimental.pallas import tpu as pltpu
from jax.sharding import PartitionSpec as P

MESH = pl.DeviceIdType.MESH
LANES = 128
ROWS = 16
HALF = 128
MATE, OWN, SLOTS = HALF, 2 * HALF, 3 * HALF
PARTS = (("own", OWN, 128), ("mate", MATE, 128), ("all", 0, 64), ("all", 64, 64))
COUNT = len(PARTS)
MOST = max(size for _, _, size in PARTS)
PIECES = 8
F32 = jnp.float32
BF16 = jnp.bfloat16


def twiddled_tables():
    k = np.arange(ROWS)[:, None, None]
    n = np.arange(LANES)[None, :, None]
    m = np.arange(LANES)[None, None, :]
    points = 2 * ROWS * LANES
    turns = (n * (2 * (k + 2 * ROWS * m) + 1)) % (2 * points)
    angle = turns * (math.pi / points)
    cos, sin = np.cos(angle), np.sin(angle)
    ahead = np.concatenate(
        [np.concatenate([cos, -sin], axis=2), np.concatenate([sin, cos], axis=2)], axis=1
    )
    return ahead.astype(BF16), np.swapaxes(ahead, 1, 2).astype(BF16)


def split_rows(rows):
    count = len(rows)
    if count == 2:
        turned = rows[1] * math.cos(math.pi / 4)
        return [(rows[0] + turned, -turned), (rows[0] - turned, -turned)]
    even, odd = split_rows(rows[0::2]), split_rows(rows[1::2])
    out = [None] * count
    for k in range(count // 2):
        angle = math.pi * (2 * k + 1) / (2 * count)
        wr, wi = math.cos(angle), -math.sin(angle)
        (er, ei), (pr, pi) = even[k], odd[k]
        tr, ti = wr * pr - wi * pi, wr * pi + wi * pr
        out[k] = (er + tr, ei + ti)
        out[count - 1 - k] = (er - tr, ti - ei)
    return out


def merge_rows(spec):
    count = len(spec)
    if count == 2:
        (a, b), (c, d) = spec
        return [a + c, (a - c - b - d) * math.cos(math.pi / 4)]
    even, odd = [], []
    for k in range(count // 2):
        angle = math.pi * (2 * k + 1) / (2 * count)
        wr, wi = math.cos(angle), -math.sin(angle)
        (pr, pi), (qr, qi) = spec[k], spec[count - 1 - k]
        dr, di = pr - qr, pi + qi
        even.append((pr + qr, pi - qi))
        odd.append((wr * dr + wi * di, wr * di - wi * dr))
    out = [None] * count
    out[0::2], out[1::2] = merge_rows(even), merge_rows(odd)
    return out


def kernel(
    scale,
    u_ref, a_ref, b_ref, h_ref, ahead_ref, back_ref,
    y_ref, f_ref,
    a_buf, b_buf, g_buf, h_buf, h_piece, h_mate, u_recv, g_recv, h_first, h_spec, first, last, y_buf,
    f_buf, f_recv, f_give, f_take, f_send, f_last,
    local_sem, h_send, h_sem, u_send, u_sem, g_send, g_sem, y_send, y_sem,
    s1, r1, s2, r2, s3, r3,
):
    own = f_ref.shape[0]
    dp, me = lax.axis_index("dp"), lax.axis_index("ctx")
    core, z_hi, x = dp % 2, (dp // 2) % 2, dp // 4
    side = (me // 2) % 2
    piece = x * 2 + core

    def cousin(step):
        return ((x ^ (step // 2)) * 4 + z_hi * 2 + (core ^ (step % 2)), me)

    other_z = (dp + 2 - 4 * z_hi, me)
    across = (dp + 2 - 4 * z_hi, me ^ 2)

    def each_step(run):
        @pl.loop(1, ROWS)
        def _(step):
            run(step)

    def near_step(run):
        @pl.loop(1, ROWS // 2)
        def _(at):
            run((at // 2) * 4 + at % 2)

    barrier = pltpu.get_barrier_semaphore()

    def greet(peer):
        pl.semaphore_signal(barrier, inc=1, device_id=peer, device_id_type=MESH)

    each_step(lambda step: greet((dp, me ^ step)))
    for peer in [other_z, across] + [cousin(step) for step in range(1, PIECES)]:
        greet(peer)

    def kept(name, size, base):
        owner = me ^ 2 if name == "mate" else me
        return pl.ds(owner * own + base, size)

    def base_of(name, slot):
        return slot - OWN + HALF if name == "own" else slot

    height = HALF // PIECES
    load_piece = pltpu.make_async_copy(
        h_ref.at[pl.ds(HALF + piece * height, height)], h_piece, local_sem.at[3 + 3 * COUNT]
    )
    load_piece.start()
    loads = [
        pltpu.make_async_copy(a_ref, a_buf, local_sem.at[0]),
        pltpu.make_async_copy(b_ref, b_buf, local_sem.at[1]),
        pltpu.make_async_copy(h_ref, h_buf, local_sem.at[2]),
    ]
    keep_u = [
        pltpu.make_async_copy(
            u_ref.at[kept(name, size, base_of(name, slot))],
            u_recv.at[me, pl.ds(slot, size)],
            local_sem.at[3 + part],
        )
        for part, (name, slot, size) in enumerate(PARTS)
    ]
    for copy in loads + keep_u:
        copy.start()
    pl.semaphore_wait(barrier, ROWS - 1 + 2 + PIECES - 1)

    def exchange(src, dst, send, recv, part, step):
        name, slot, size = PARTS[part]
        owner = me ^ step ^ 2 if name == "mate" else me ^ step
        return pltpu.make_async_remote_copy(
            src_ref=src.at[pl.ds(owner * own + base_of(name, slot), size)],
            dst_ref=dst.at[me, pl.ds(slot, size)],
            send_sem=send.at[part, step],
            recv_sem=recv.at[part, step],
            device_id=(dp, me ^ step),
            device_id_type=MESH,
        )

    def move_u(part, step):
        return exchange(u_ref, u_recv, u_send, u_sem, part, step)

    def move_g(part, step):
        return exchange(g_buf, g_recv, g_send, g_sem, part, step)

    def move_y(part, step):
        name, slot, size = PARTS[part]
        return pltpu.make_async_remote_copy(
            src_ref=y_buf.at[me ^ step, pl.ds(slot, size)],
            dst_ref=y_ref.at[kept(name, size, base_of(name, slot))],
            send_sem=y_send.at[part, step],
            recv_sem=y_sem.at[part, step],
            device_id=(dp, me ^ step),
            device_id_type=MESH,
        )

    def steps_of(part):
        return each_step if PARTS[part][0] == "all" else near_step

    load_piece.wait()
    for j in range(ROWS):
        lanes = slice(j * LANES, (j + 1) * LANES)
        h_mate[1, :height, lanes] = h_piece[:, lanes].astype(BF16)

    give_h = pltpu.make_async_remote_copy(
        src_ref=h_mate.at[1, pl.ds(0, height)],
        dst_ref=h_mate.at[0, pl.ds(piece * height, height)],
        send_sem=h_send.at[0], recv_sem=h_sem.at[0],
        device_id=across, device_id_type=MESH,
    )
    give_h.start()

    def share_h(step):
        rows = pl.ds(piece * height, height)
        return pltpu.make_async_remote_copy(
            src_ref=h_mate.at[0, rows], dst_ref=h_mate.at[0, rows],
            send_sem=h_send.at[step], recv_sem=h_sem.at[step],
            device_id=cousin(step), device_id_type=MESH,
        )

    near_step(lambda step: move_u(0, step).start())
    loads[0].wait()
    loads[1].wait()

    def make_g(begin, size):
        rows = pl.ds(begin, size)
        g_buf[rows] = (a_buf[rows].astype(F32) * b_buf[rows].astype(F32)).astype(BF16)

    def first_g(step):
        make_g((me ^ step) * own + HALF, own - HALF)
        move_g(0, step).start()
    each_step(first_g)
    make_g(me * own + HALF, own - HALF)

    def send_part(part, also=None):
        @pl.loop(0, ROWS // 2)
        def _(at):
            step = (at // 2) * 4 + at % 2
            move_g(part, step + 2).start()
            if PARTS[part][0] == "all":
                move_u(part, step + 2).start()

            @pl.when(at > 0)
            def _():
                move_u(part, step).start()
                move_g(part, step).start()
                if also is not None:
                    move_y(also, step).start()

    give_h.wait_recv()
    for step in range(1, PIECES):
        share_h(step).start()
    send_part(1)

    @pl.loop(0, ROWS)
    def _(to):
        make_g(to * own, HALF)
    send_part(2)
    keep_g = [
        pltpu.make_async_copy(
            g_buf.at[kept(name, size, base_of(name, slot))],
            g_recv.at[me, pl.ds(slot, size)],
            local_sem.at[3 + COUNT + part],
        )
        for part, (name, slot, size) in enumerate(PARTS)
    ]
    for copy in keep_g:
        copy.start()

    @pl.loop(0, ROWS // 2)
    def _(at):
        u_recv[(at // 2) * 4 + 2 * (1 - side) + at % 2, HALF:] = jnp.zeros((SLOTS - HALF, LANES), BF16)

    loads[2].wait()
    @pl.loop(0, own // 16)
    def _(at):
        rows = pl.ds(at * 16, 16)
        put = pl.ds(at * 16 + (at // (HALF // 16)) * HALF, 16)
        spec = split_rows([h_buf[rows, j * LANES : (j + 1) * LANES] for j in range(ROWS)])
        for k, (re, im) in enumerate(spec):
            h_first[k, put, :LANES] = re.astype(BF16)
            h_first[k, put, LANES:] = im.astype(BF16)

    def spectrum(begin, size):
        @pl.loop(0, ROWS)
        def _(k):
            rows = pl.ds(begin, size)
            h_spec[k, rows] = jnp.dot(
                h_first[k, rows], ahead_ref[k], preferred_element_type=F32
            ) * (1.0 / (ROWS * LANES))

    spectrum(0, HALF)
    spectrum(OWN, HALF)

    def mate_taps():
        for step in range(1, PIECES):
            share_h(step).wait_recv()

        @pl.loop(0, HALF // 16)
        def _(at):
            rows = pl.ds(at * 16, 16)
            put = pl.ds(MATE + at * 16, 16)
            spec = split_rows(
                [h_mate[0, rows, j * LANES : (j + 1) * LANES].astype(F32) for j in range(ROWS)]
            )
            for k, (re, im) in enumerate(spec):
                h_first[k, put, :LANES] = re.astype(BF16)
                h_first[k, put, LANES:] = im.astype(BF16)
        spectrum(MATE, HALF)

    def compute(part):
        name, base, size = PARTS[part]

        @pl.loop(0, size // 16)
        def _(at):
            rows = pl.ds(base + at * 16, 16)
            for place, source in enumerate((g_recv, u_recv)):
                spec = split_rows([source[j, rows].astype(F32) for j in range(ROWS)])
                put = pl.ds(place * size + at * 16, 16)
                for k, (re, im) in enumerate(spec):
                    first[k, put, :LANES] = re.astype(BF16)
                    first[k, put, LANES:] = im.astype(BF16)

        @pl.loop(0, ROWS, unroll=2)
        def _(k):
            spec = jnp.dot(first[k, : 2 * size], ahead_ref[k], preferred_element_type=F32)
            gr, gi = spec[:size, :LANES], spec[:size, LANES:]
            ur, ui = spec[size:, :LANES], spec[size:, LANES:]
            hr = h_spec[k, pl.ds(base, size), :LANES]
            hi = h_spec[k, pl.ds(base, size), LANES:]
            to_input = jnp.concatenate([hr * gr + hi * gi, hr * gi - hi * gr], axis=1)
            to_filter = jnp.concatenate([gr * ur + gi * ui, gi * ur - gr * ui], axis=1)
            both = jnp.concatenate([to_input, to_filter], axis=0).astype(BF16)
            last[k, : 2 * size] = jnp.dot(both, back_ref[k], preferred_element_type=F32)

        @pl.loop(0, size // 16)
        def _(at):
            rows = pl.ds(base + at * 16, 16)
            for place in range(2):
                take = pl.ds(place * size + at * 16, 16)
                out = merge_rows([(last[k, take, :LANES], last[k, take, LANES:]) for k in range(ROWS)])
                for j in range(ROWS):
                    if place == 0:
                        y_buf[j, rows] = out[j].astype(BF16)
                    else:
                        f_buf[(j // 4) * 2 + j % 2, (j // 2) % 2, rows] = out[j].astype(BF16)

    def slots(part):
        return pl.ds(PARTS[part][1], PARTS[part][2])

    def sum_cousins(part, step):
        return pltpu.make_async_remote_copy(
            src_ref=f_buf.at[piece ^ step, :, slots(part)],
            dst_ref=f_recv.at[step, :, slots(part)],
            send_sem=s1.at[part, step], recv_sem=r1.at[part, step],
            device_id=cousin(step), device_id_type=MESH,
        )

    sum_mate = pltpu.make_async_remote_copy(
        src_ref=f_give, dst_ref=f_take, send_sem=s2, recv_sem=r2,
        device_id=across, device_id_type=MESH,
    )

    def sum_z(part):
        return pltpu.make_async_remote_copy(
            src_ref=f_send.at[slots(part)], dst_ref=f_last.at[slots(part)],
            send_sem=s3.at[part], recv_sem=r3.at[part],
            device_id=other_z, device_id_type=MESH,
        )

    def held(part, half):
        name, slot, size = PARTS[part]
        total = f_buf[piece, half, slots(part)].astype(F32)
        for step in range(1, PIECES):
            total = total + f_recv[step, half, slots(part)].astype(F32)
        if name == "own":
            total = total + f_take[half].astype(F32)
        return total

    def after_cousins(part):
        for step in range(1, PIECES):
            sum_cousins(part, step).wait()
        name = PARTS[part][0]
        if name == "mate":
            for half in range(2):
                f_give[half] = held(part, half).astype(BF16)
            sum_mate.start()
        else:
            if name == "own":
                sum_mate.wait()
            f_send[slots(part)] = held(part, 1 - z_hi).astype(BF16)
            sum_z(part).start()

    def after_z(part):
        name, slot, size = PARTS[part]
        sum_z(part).wait()
        f_ref[pl.ds(base_of(name, slot), size)] = (
            held(part, z_hi) + f_last[slots(part)].astype(F32)
        ) * scale

    def keep_y(part):
        name, slot, size = PARTS[part]
        return pltpu.make_async_copy(
            y_buf.at[me, pl.ds(slot, size)],
            y_ref.at[kept(name, size, base_of(name, slot))],
            local_sem.at[3 + 2 * COUNT + part],
        )

    def begin(part):
        each_step(lambda step: move_g(part, step).wait_recv())
        steps_of(part)(lambda step: move_u(part, step).wait_recv())
        keep_g[part].wait()
        keep_u[part].wait()
        if PARTS[part][0] == "mate":
            mate_taps()
        compute(part)
        for step in range(1, PIECES):
            sum_cousins(part, step).start()
        keep_y(part).start()

    begin(0)
    send_part(3, also=0)
    begin(1)
    begin(2)
    each_step(lambda step: move_y(2, step).start())
    near_step(lambda step: move_y(1, step).start())
    after_cousins(1)
    begin(3)
    each_step(lambda step: move_y(3, step).start())
    after_cousins(0)
    after_cousins(2)
    after_cousins(3)
    after_z(0)
    after_z(2)
    after_z(3)

    give_h.wait_send()
    for step in range(1, PIECES):
        share_h(step).wait_send()
    for part in range(COUNT):
        keep_y(part).wait()
        each_step(lambda step: move_g(part, step).wait_send())

        def finish(step):
            move_u(part, step).wait_send()
            move_y(part, step).wait()
        steps_of(part)(finish)


def on_device(saved_input, out_gate, grad_out, long_filter):
    _, channels, width = saved_input.shape
    own, length = long_filter.shape
    scale = 1.0 / (math.sqrt(lax.axis_size("dp") * length) * ROWS * LANES)
    ahead, back = twiddled_tables()
    in_hbm = pl.BlockSpec(memory_space=pl.ANY)
    in_vmem = pl.BlockSpec(memory_space=pltpu.VMEM)
    dma = pltpu.SemaphoreType.DMA

    def run(*operands):
        return pl.pallas_call(
            lambda *refs: kernel(scale, *refs),
            out_shape=(
                jax.ShapeDtypeStruct((channels, width), BF16),
                jax.ShapeDtypeStruct((own, width), F32),
            ),
            in_specs=[in_hbm] * 4 + [in_vmem] * 2,
            out_specs=(in_hbm, in_vmem),
            scratch_shapes=[
                pltpu.VMEM((channels, width), BF16),
                pltpu.VMEM((channels, width), BF16),
                pltpu.VMEM((channels, width), BF16),
                pltpu.VMEM((own, length), F32),
                pltpu.VMEM((HALF // PIECES, length), F32),
                pltpu.VMEM((2, HALF, length), BF16),
                pltpu.VMEM((ROWS, SLOTS, width), BF16),
                pltpu.VMEM((ROWS, SLOTS, width), BF16),
                pltpu.VMEM((ROWS, SLOTS, 2 * LANES), BF16),
                pltpu.VMEM((ROWS, SLOTS, 2 * LANES), F32),
                pltpu.VMEM((ROWS, 2 * MOST, 2 * LANES), BF16),
                pltpu.VMEM((ROWS, 2 * MOST, 2 * LANES), F32),
                pltpu.VMEM((ROWS, SLOTS, width), BF16),
                pltpu.VMEM((PIECES, 2, SLOTS, LANES), BF16),
                pltpu.VMEM((PIECES, 2, SLOTS, LANES), BF16),
                pltpu.VMEM((2, HALF, LANES), BF16),
                pltpu.VMEM((2, HALF, LANES), BF16),
                pltpu.VMEM((SLOTS, LANES), BF16),
                pltpu.VMEM((SLOTS, LANES), BF16),
                dma((4 + 3 * COUNT,)),
                dma((PIECES,)), dma((PIECES,)),
                dma((COUNT, ROWS)), dma((COUNT, ROWS)),
                dma((COUNT, ROWS)), dma((COUNT, ROWS)),
                dma((COUNT, ROWS)), dma((COUNT, ROWS)),
                dma((COUNT, PIECES)), dma((COUNT, PIECES)),
                dma, dma,
                dma((COUNT,)), dma((COUNT,)),
            ],
            compiler_params=pltpu.CompilerParams(
                collective_id=0, has_side_effects=True, vmem_limit_bytes=56 * 2**20
            ),
        )(*operands)

    grad_input, grad_filter = run(
        saved_input[0], out_gate[0], grad_out[0], long_filter, jnp.asarray(ahead), jnp.asarray(back)
    )
    return grad_input[None], grad_filter


def solution(mesh):
    in_specs = (P("dp", None, "ctx"), P("dp", None, "ctx"), P("dp", None, "ctx"), P("ctx", None))
    out_specs = (P("dp", None, "ctx"), P("ctx", "dp"))
    return jax.shard_map(
        on_device, mesh=mesh, in_specs=in_specs, out_specs=out_specs, check_vma=False
    )
```

time: 92.4 us -> 84.2 us (0.911)
  the two profiles are of different devices: /device:TPU:6 before, /device:TPU:26 now
where the time goes in v2:
time: 84.2 us; the launch traced here: 83.4 us
  Pallas kernels  79.8 us (95%)
  local copies, waits for them, and re-layouts  2.96 us (4%)
    pallas_call x1, Pallas kernels, run(): pl.pallas_call(lambda *refs: kernel(scale, *refs), out_shape=(jax.ShapeDt...  79.8 us
    unnamed x4, local copies, waits for them, and re-layouts  2.96 us

profile of v2, /device:TPU:26, one launch (start us, length us, event | category | flops | bytes accessed | tf_op | source)
XLA Modules:
  0.0 83.4 jit_solution(7858003242604407734)
XLA Ops:
  0.6 79.8 %shard_map.77 = (bf16[4096,128]{1,0:T(8,128)(2,1)}, f32[256,128]{1,0:T(8,128)}) custom-call(bf16[4096,128]{1,0:T(8,128)(2,1)} %bitcast.4, bf16[4096,128]{1,0:T(8,128)(2,1)} %bitcast.5, bf16[4096,128]{1,0:T(8,128)(2,1)} %bitcast.6, f32[256,2048]{1,0:T(8,128)} %refs_3_.1, bf16[16,256,256]{2,1,0:T(8,128)(2,1)} %constant.4.clone.refs_4_, ...), custom_call_target="tpu_custom_call" | custom-call | tf_op jit(solution)/shard_map/pallas_call | solution.py:434
  80.4 0.0 copy-start
  80.4 2.3 %copy.10 = bf16[1,4096,128]{2,1,0:T(8,128)(2,1)} copy(bf16[1,4096,128]{2,1,0:T(8,128)(2,1)} %bitcast.7) | data formatting | bytes 2097152
  82.7 0.0 copy-done
  82.7 0.7 copy.11
Async XLA Ops:
  80.4 2.3 %copy-start = (f32[256,128]{1,0:T(8,128)S(1)}, f32[256,128]{1,0:T(8,128)}, u32[]{:S(2)}) copy-start(f32[256,128]{1,0:T(8,128)} %get-tuple-element.9) | copy-start | bytes 393220

commit v3 on v2

--- a/solution.py
+++ b/solution.py
@@ -145,8 +145,8 @@
         return pltpu.make_async_remote_copy(
             src_ref=src.at[pl.ds(owner * own + base_of(name, slot), size)],
             dst_ref=dst.at[me, pl.ds(slot, size)],
-            send_sem=send.at[part, step],
-            recv_sem=recv.at[part, step],
+            send_sem=send.at[part],
+            recv_sem=recv.at[part],
             device_id=(dp, me ^ step),
             device_id_type=MESH,
         )
@@ -162,14 +162,19 @@
         return pltpu.make_async_remote_copy(
             src_ref=y_buf.at[me ^ step, pl.ds(slot, size)],
             dst_ref=y_ref.at[kept(name, size, base_of(name, slot))],
-            send_sem=y_send.at[part, step],
-            recv_sem=y_sem.at[part, step],
+            send_sem=y_send.at[part],
+            recv_sem=y_sem.at[part],
             device_id=(dp, me ^ step),
             device_id_type=MESH,
         )
 
-    def steps_of(part):
-        return each_step if PARTS[part][0] == "all" else near_step
+    def all_of(ref, sem):
+        pltpu.make_async_copy(ref, ref, sem).wait()
+
+    def blocks(part, whole=False):
+        name, slot, size = PARTS[part]
+        count = ROWS - 1 if whole or name == "all" else ROWS // 2 - 1
+        return g_recv.at[pl.ds(0, count), pl.ds(slot, size)]
 
     load_piece.wait()
     for j in range(ROWS):
@@ -188,7 +193,7 @@
         rows = pl.ds(piece * height, height)
         return pltpu.make_async_remote_copy(
             src_ref=h_mate.at[0, rows], dst_ref=h_mate.at[0, rows],
-            send_sem=h_send.at[step], recv_sem=h_sem.at[step],
+            send_sem=h_send.at[1], recv_sem=h_sem.at[1],
             device_id=cousin(step), device_id_type=MESH,
         )
 
@@ -267,8 +272,7 @@
     spectrum(OWN, HALF)
 
     def mate_taps():
-        for step in range(1, PIECES):
-            share_h(step).wait_recv()
+        all_of(h_mate.at[0, pl.ds(0, (PIECES - 1) * height)], h_sem.at[1])
 
         @pl.loop(0, HALF // 16)
         def _(at):
@@ -326,7 +330,7 @@
         return pltpu.make_async_remote_copy(
             src_ref=f_buf.at[piece ^ step, :, slots(part)],
             dst_ref=f_recv.at[step, :, slots(part)],
-            send_sem=s1.at[part, step], recv_sem=r1.at[part, step],
+            send_sem=s1.at[part], recv_sem=r1.at[part],
             device_id=cousin(step), device_id_type=MESH,
         )
 
@@ -352,8 +356,7 @@
         return total
 
     def after_cousins(part):
-        for step in range(1, PIECES):
-            sum_cousins(part, step).wait()
+        all_of(f_recv.at[pl.ds(1, PIECES - 1), :, slots(part)], r1.at[part])
         name = PARTS[part][0]
         if name == "mate":
             for half in range(2):
@@ -381,8 +384,8 @@
         )
 
     def begin(part):
-        each_step(lambda step: move_g(part, step).wait_recv())
-        steps_of(part)(lambda step: move_u(part, step).wait_recv())
+        all_of(blocks(part, True), g_sem.at[part])
+        all_of(blocks(part), u_sem.at[part])
         keep_g[part].wait()
         keep_u[part].wait()
         if PARTS[part][0] == "mate":
@@ -409,16 +412,14 @@
     after_z(3)
 
     give_h.wait_send()
-    for step in range(1, PIECES):
-        share_h(step).wait_send()
+    all_of(h_mate.at[0, pl.ds(0, (PIECES - 1) * height)], h_send.at[1])
     for part in range(COUNT):
         keep_y(part).wait()
-        each_step(lambda step: move_g(part, step).wait_send())
-
-        def finish(step):
-            move_u(part, step).wait_send()
-            move_y(part, step).wait()
-        steps_of(part)(finish)
+        all_of(f_recv.at[pl.ds(1, PIECES - 1), :, slots(part)], s1.at[part])
+        all_of(blocks(part, True), g_send.at[part])
+        all_of(blocks(part), u_send.at[part])
+        all_of(blocks(part), y_send.at[part])
+        all_of(blocks(part), y_sem.at[part])
 
 
 def on_device(saved_input, out_gate, grad_out, long_filter):
@@ -460,11 +461,11 @@
                 pltpu.VMEM((SLOTS, LANES), BF16),
                 pltpu.VMEM((SLOTS, LANES), BF16),
                 dma((4 + 3 * COUNT,)),
-                dma((PIECES,)), dma((PIECES,)),
-                dma((COUNT, ROWS)), dma((COUNT, ROWS)),
-                dma((COUNT, ROWS)), dma((COUNT, ROWS)),
-                dma((COUNT, ROWS)), dma((COUNT, ROWS)),
-                dma((COUNT, PIECES)), dma((COUNT, PIECES)),
+                dma((2,)), dma((2,)),
+                dma((COUNT,)), dma((COUNT,)),
+                dma((COUNT,)), dma((COUNT,)),
+                dma((COUNT,)), dma((COUNT,)),
+                dma((COUNT,)), dma((COUNT,)),
                 dma, dma,
                 dma((COUNT,)), dma((COUNT,)),
             ],

time: 84.2 us -> 79.4 us (0.943)
  Pallas kernels: 79.8 us -> 75.1 us
    pallas_call x1, Pallas kernels: 79.8 us -> 75.1 us  [run(): pl.pallas_call(lambda *refs: kernel(scale, *refs), out_shape=(jax.ShapeDt...]
where the time goes in v3:
time: 79.4 us; the launch traced here: 78.7 us
  Pallas kernels  75.1 us (95%)
  local copies, waits for them, and re-layouts  2.96 us (4%)
    pallas_call x1, Pallas kernels, run(): pl.pallas_call(lambda *refs: kernel(scale, *refs), out_shape=(jax.ShapeDt...  75.1 us
    unnamed x4, local copies, waits for them, and re-layouts  2.96 us

profile of v3, /device:TPU:26, one launch (start us, length us, event | category | flops | bytes accessed | tf_op | source)
XLA Modules:
  0.0 78.7 jit_solution(11914046983689816696)
XLA Ops:
  0.6 75.1 %shard_map.77 = (bf16[4096,128]{1,0:T(8,128)(2,1)}, f32[256,128]{1,0:T(8,128)}) custom-call(bf16[4096,128]{1,0:T(8,128)(2,1)} %bitcast.4, bf16[4096,128]{1,0:T(8,128)(2,1)} %bitcast.5, bf16[4096,128]{1,0:T(8,128)(2,1)} %bitcast.6, f32[256,2048]{1,0:T(8,128)} %refs_3_.1, bf16[16,256,256]{2,1,0:T(8,128)(2,1)} %constant.4.clone.refs_4_, ...), custom_call_target="tpu_custom_call" | custom-call | tf_op jit(solution)/shard_map/pallas_call | solution.py:435
  75.7 0.0 copy-start
  75.8 2.3 %copy.10 = bf16[1,4096,128]{2,1,0:T(8,128)(2,1)} copy(bf16[1,4096,128]{2,1,0:T(8,128)(2,1)} %bitcast.7) | data formatting | bytes 2097152
  78.0 0.0 copy-done
  78.1 0.7 copy.11
Async XLA Ops:
  75.7 2.3 %copy-start = (f32[256,128]{1,0:T(8,128)S(1)}, f32[256,128]{1,0:T(8,128)}, u32[]{:S(2)}) copy-start(f32[256,128]{1,0:T(8,128)} %get-tuple-element.9) | copy-start | bytes 393220

commit v4 on v3

--- a/solution.py
+++ b/solution.py
@@ -72,9 +72,9 @@
 
 def kernel(
     scale,
-    u_ref, a_ref, b_ref, h_ref, ahead_ref, back_ref,
+    u_ref, a_ref, b_ref, h_ref, ahead_hbm, back_hbm,
     y_ref, f_ref,
-    a_buf, b_buf, g_buf, h_buf, h_piece, h_mate, u_recv, g_recv, h_first, h_spec, first, last, y_buf,
+    ahead_ref, back_ref, a_buf, b_buf, g_buf, h_buf, h_piece, h_mate, u_recv, g_recv, h_first, h_spec, first, last, y_buf,
     f_buf, f_recv, f_give, f_take, f_send, f_last,
     local_sem, h_send, h_sem, u_send, u_sem, g_send, g_sem, y_send, y_sem,
     s1, r1, s2, r2, s3, r3,
@@ -107,8 +107,8 @@
         pl.semaphore_signal(barrier, inc=1, device_id=peer, device_id_type=MESH)
 
     each_step(lambda step: greet((dp, me ^ step)))
-    for peer in [other_z, across] + [cousin(step) for step in range(1, PIECES)]:
-        greet(peer)
+    for step in range(1, PIECES):
+        greet(cousin(step))
 
     def kept(name, size, base):
         owner = me ^ 2 if name == "mate" else me
@@ -126,6 +126,8 @@
         pltpu.make_async_copy(a_ref, a_buf, local_sem.at[0]),
         pltpu.make_async_copy(b_ref, b_buf, local_sem.at[1]),
         pltpu.make_async_copy(h_ref, h_buf, local_sem.at[2]),
+        pltpu.make_async_copy(ahead_hbm, ahead_ref, local_sem.at[4 + 3 * COUNT]),
+        pltpu.make_async_copy(back_hbm, back_ref, local_sem.at[5 + 3 * COUNT]),
     ]
     keep_u = [
         pltpu.make_async_copy(
@@ -135,9 +137,12 @@
         )
         for part, (name, slot, size) in enumerate(PARTS)
     ]
-    for copy in loads + keep_u:
+    for copy in loads[:2]:
         copy.start()
-    pl.semaphore_wait(barrier, ROWS - 1 + 2 + PIECES - 1)
+
+    for peer in (other_z, across):
+        greet(peer)
+    pl.semaphore_wait(barrier, ROWS - 1 + PIECES - 1 + 2)
 
     def exchange(src, dst, send, recv, part, step):
         name, slot, size = PARTS[part]
@@ -197,7 +202,6 @@
             device_id=cousin(step), device_id_type=MESH,
         )
 
-    near_step(lambda step: move_u(0, step).start())
     loads[0].wait()
     loads[1].wait()
 
@@ -208,7 +212,17 @@
     def first_g(step):
         make_g((me ^ step) * own + HALF, own - HALF)
         move_g(0, step).start()
-    each_step(first_g)
+    @pl.loop(0, ROWS // 2)
+    def _(at):
+        step = (at // 2) * 4 + at % 2
+        first_g(step + 2)
+
+        @pl.when(at > 0)
+        def _():
+            first_g(step)
+            move_u(0, step).start()
+    for copy in loads[2:] + keep_u:
+        copy.start()
     make_g(me * own + HALF, own - HALF)
 
     def send_part(part, also=None):
@@ -250,7 +264,8 @@
     def _(at):
         u_recv[(at // 2) * 4 + 2 * (1 - side) + at % 2, HALF:] = jnp.zeros((SLOTS - HALF, LANES), BF16)
 
-    loads[2].wait()
+    for copy in loads[2:]:
+        copy.wait()
     @pl.loop(0, own // 16)
     def _(at):
         rows = pl.ds(at * 16, 16)
@@ -403,9 +418,9 @@
     near_step(lambda step: move_y(1, step).start())
     after_cousins(1)
     begin(3)
+    after_cousins(2)
+    after_cousins(0)
     each_step(lambda step: move_y(3, step).start())
-    after_cousins(0)
-    after_cousins(2)
     after_cousins(3)
     after_z(0)
     after_z(2)
@@ -435,12 +450,14 @@
         return pl.pallas_call(
             lambda *refs: kernel(scale, *refs),
             out_shape=(
-                jax.ShapeDtypeStruct((channels, width), BF16),
-                jax.ShapeDtypeStruct((own, width), F32),
+                pltpu.VMEM((channels, width), BF16),
+                pltpu.VMEM((own, width), F32),
             ),
-            in_specs=[in_hbm] * 4 + [in_vmem] * 2,
-            out_specs=(in_hbm, in_vmem),
+            in_specs=[in_hbm] * 6,
+            out_specs=(in_vmem, in_vmem),
             scratch_shapes=[
+                pltpu.VMEM(ahead.shape, BF16),
+                pltpu.VMEM(back.shape, BF16),
                 pltpu.VMEM((channels, width), BF16),
                 pltpu.VMEM((channels, width), BF16),
                 pltpu.VMEM((channels, width), BF16),
@@ -460,7 +477,7 @@
                 pltpu.VMEM((2, HALF, LANES), BF16),
                 pltpu.VMEM((SLOTS, LANES), BF16),
                 pltpu.VMEM((SLOTS, LANES), BF16),
-                dma((4 + 3 * COUNT,)),
+                dma((6 + 3 * COUNT,)),
                 dma((2,)), dma((2,)),
                 dma((COUNT,)), dma((COUNT,)),
                 dma((COUNT,)), dma((COUNT,)),
@@ -470,7 +487,7 @@
                 dma((COUNT,)), dma((COUNT,)),
             ],
             compiler_params=pltpu.CompilerParams(
-                collective_id=0, has_side_effects=True, vmem_limit_bytes=56 * 2**20
+                collective_id=0, has_side_effects=True, vmem_limit_bytes=58 * 2**20
             ),
         )(*operands)
 

time: 79.4 us -> 75.3 us (0.948)
  Pallas kernels: 75.1 us -> 72.6 us
  local copies, waits for them, and re-layouts: 2.96 us -> 1.63 us
    pallas_call x1, Pallas kernels: 75.1 us -> 72.6 us  [run(): pl.pallas_call(lambda *refs: kernel(scale, *refs), out_shape=(pltpu.VMEM(...]
    unnamed x4 -> x2, local copies, waits for them, and re-layouts: 2.96 us -> 1.63 us
where the time goes in v4:
time: 75.3 us; the launch traced here: 74.9 us
  Pallas kernels  72.6 us (96%)
  local copies, waits for them, and re-layouts  1.63 us (2%)
    pallas_call x1, Pallas kernels, run(): pl.pallas_call(lambda *refs: kernel(scale, *refs), out_shape=(pltpu.VMEM(...  72.6 us
    unnamed x2, local copies, waits for them, and re-layouts  1.63 us

profile of v4, /device:TPU:26, one launch (start us, length us, event | category | flops | bytes accessed | tf_op | source)
XLA Modules:
  0.0 74.9 jit_solution(15612447925654387994)
XLA Ops:
  0.6 72.6 %shard_map.77 = (bf16[4096,128]{1,0:T(8,128)(2,1)S(1)}, f32[256,128]{1,0:T(8,128)S(1)}) custom-call(bf16[4096,128]{1,0:T(8,128)(2,1)} %bitcast.5, bf16[4096,128]{1,0:T(8,128)(2,1)} %bitcast.6, bf16[4096,128]{1,0:T(8,128)(2,1)} %bitcast.7, f32[256,2048]{1,0:T(8,128)} %refs_3_.1, bf16[16,256,256]{2,1,0:T(8,128)(2,1)} %constant.4.clone.refs_4_, ...), custom_call_target="tpu_custom_call" | custom-call | tf_op jit(solution)/shard_map/pallas_call | solution.py:450
  73.2 1.0 %copy.10 = bf16[1,4096,128]{2,1,0:T(8,128)(2,1)} copy(bf16[1,4096,128]{2,1,0:T(8,128)(2,1)S(1)} %bitcast.4) | data formatting | bytes 2097152
  74.2 0.7 copy.11

commit v5 on v4

--- a/solution.py
+++ b/solution.py
@@ -326,17 +326,19 @@
             both = jnp.concatenate([to_input, to_filter], axis=0).astype(BF16)
             last[k, : 2 * size] = jnp.dot(both, back_ref[k], preferred_element_type=F32)
 
+    def merge(part, place):
+        name, base, size = PARTS[part]
+
         @pl.loop(0, size // 16)
         def _(at):
             rows = pl.ds(base + at * 16, 16)
-            for place in range(2):
-                take = pl.ds(place * size + at * 16, 16)
-                out = merge_rows([(last[k, take, :LANES], last[k, take, LANES:]) for k in range(ROWS)])
-                for j in range(ROWS):
-                    if place == 0:
-                        y_buf[j, rows] = out[j].astype(BF16)
-                    else:
-                        f_buf[(j // 4) * 2 + j % 2, (j // 2) % 2, rows] = out[j].astype(BF16)
+            take = pl.ds(place * size + at * 16, 16)
+            out = merge_rows([(last[k, take, :LANES], last[k, take, LANES:]) for k in range(ROWS)])
+            for j in range(ROWS):
+                if place == 0:
+                    y_buf[j, rows] = out[j].astype(BF16)
+                else:
+                    f_buf[(j // 4) * 2 + j % 2, (j // 2) % 2, rows] = out[j].astype(BF16)
 
     def slots(part):
         return pl.ds(PARTS[part][1], PARTS[part][2])
@@ -406,8 +408,10 @@
         if PARTS[part][0] == "mate":
             mate_taps()
         compute(part)
+        merge(part, 1)
         for step in range(1, PIECES):
             sum_cousins(part, step).start()
+        merge(part, 0)
         keep_y(part).start()
 
     begin(0)

time: 75.3 us -> 75.1 us (level)
  no operation moved by 1% of the time
where the time goes in v5:
time: 75.1 us; the launch traced here: 75 us
  Pallas kernels  72.8 us (97%)
  local copies, waits for them, and re-layouts  1.63 us (2%)
    pallas_call x1, Pallas kernels, run(): pl.pallas_call(lambda *refs: kernel(scale, *refs), out_shape=(pltpu.VMEM(...  72.8 us
    unnamed x2, local copies, waits for them, and re-layouts  1.63 us

profile of v5, /device:TPU:26, one launch (start us, length us, event | category | flops | bytes accessed | tf_op | source)
XLA Modules:
  0.0 75.0 jit_solution(12732970679994079819)
XLA Ops:
  0.6 72.8 %shard_map.77 = (bf16[4096,128]{1,0:T(8,128)(2,1)S(1)}, f32[256,128]{1,0:T(8,128)S(1)}) custom-call(bf16[4096,128]{1,0:T(8,128)(2,1)} %bitcast.5, bf16[4096,128]{1,0:T(8,128)(2,1)} %bitcast.6, bf16[4096,128]{1,0:T(8,128)(2,1)} %bitcast.7, f32[256,2048]{1,0:T(8,128)} %refs_3_.1, bf16[16,256,256]{2,1,0:T(8,128)(2,1)} %constant.4.clone.refs_4_, ...), custom_call_target="tpu_custom_call" | custom-call | tf_op jit(solution)/shard_map/pallas_call | solution.py:454
  73.4 1.0 %copy.10 = bf16[1,4096,128]{2,1,0:T(8,128)(2,1)} copy(bf16[1,4096,128]{2,1,0:T(8,128)(2,1)S(1)} %bitcast.4) | data formatting | bytes 2097152
  74.4 0.7 copy.11
